TPU v7x, 32 devices: a whole 2x2x4 slice. The times are simulated.
32 devices in a mesh: groups: 2 (over y), gx: 4 (over z), gy: 2 (over x), gz: 2 (over core).
Axes of the slice: x: 2, y: 2, z: 4, core: 2. Of those that a mesh axis runs over, the one named last changes fastest.
Arguments:
- adjoint_source: float32 [5, 4, 4, 4, 8, 2, 256], P(None, None, None, None, ('groups', 'gx'), 'gy', 'gz'), parts along dimension 4, may hold values from -6 to 6
- diagonal: bfloat16 [5, 4, 4, 4, 8, 2, 256], P(None, None, None, None, ('groups', 'gx'), 'gy', 'gz'), parts along dimension 4, may hold values from 2 to 4
- volume_coupling: bfloat16 [3, 5, 5, 4, 4, 4, 8, 2, 256], P(None, None, None, None, None, None, ('groups', 'gx'), 'gy', 'gz'), parts along dimension 6, may hold values from -0.5 to 0.5
- surface_coupling: bfloat16 [6, 5, 5, 4, 4, 8, 2, 256], P(None, None, None, None, None, ('groups', 'gx'), 'gy', 'gz'), parts along dimension 5, may hold values from -1.1953125 to 1.1953125
- mortar_owner: int32 [2048, 1], P(('groups', 'gx', 'gy', 'gz')), parts along dimension 0, may hold values from 0 to 3, as said below
- mortar_fine: int32 [2048], P(('groups', 'gx', 'gy', 'gz')), parts along dimension 0, may hold values from 0 to 127, as said below
- mortar_coarse: int32 [2048], P(('groups', 'gx', 'gy', 'gz')), parts along dimension 0, may hold values from 0 to 127, as said below
- mortar_quarter: int32 [2048], P(('groups', 'gx', 'gy', 'gz')), parts along dimension 0, may hold values from 0 to 3
- mortar_side: int32 [2048], P(('groups', 'gx', 'gy', 'gz')), parts along dimension 0, may hold values from 0 to 5
- mortar_coupling: float32 [2048, 2, 5, 5], P(('groups', 'gx', 'gy', 'gz')), parts along dimension 0, may hold values from -2.4 to 2.4
Outputs:
- adjoint_field: float32 [5, 4, 4, 4, 8, 2, 256], P(None, None, None, None, ('groups', 'gx'), 'gy', 'gz'), parts along dimension 4
There are 2 independent parts, one for each index of `groups`. A program takes and returns all parts, laid end to end along the dimension named above; each array names one. Nothing has to cross between parts.
Inputs may be any that keep to these rules, and one draw needn't show every extreme that they name: `mortar_owner`: the owner index of a row is the first-dimension index of the row's device or one beside it; within the rows of one device (aligned blocks of 64 rows) no owner index is named by more than 32 rows, and some owner index is named by exactly 32 rows. `mortar_fine`: where the owner is the device below along the first dimension, the fine element lies in the device's first element layer along that dimension and the face is 0; where it is the device above, in the last layer and the face is 1. `mortar_coarse`: where the owner differs from the row's device, the coarse element lies across the face from the fine element, in the owner's facing element layer.
All inputs are finite; a program needn't handle non-finite values.
Results may differ from a plain program's by a relative error of at most 0.0003.
Values sent between devices are 32-bit elements; how exact they have to be, the bound alone decides.
A program may use at most 64 MiB of HBM per device.

v0:
```python
import functools

import jax
import jax.numpy as jnp
import ml_dtypes
import numpy as np
from jax import lax
from jax.experimental import pallas as pl
from jax.experimental.pallas import tpu as pltpu
from jax.sharding import PartitionSpec as P

KRYLOV = 4
SHIFT = 3.0
F32 = jnp.float32
BF16 = jnp.bfloat16
LANES = 128
MESH = pl.DeviceIdType.MESH


def node_tables():
    points = np.array([-1.0, -1.0 / np.sqrt(5.0), 1.0 / np.sqrt(5.0), 1.0])
    barycentric = np.array(
        [1.0 / np.prod([points[m] - points[k] for k in range(4) if k != m]) for m in range(4)]
    )
    derivative = np.zeros((4, 4))
    for i in range(4):
        for m in range(4):
            if i != m:
                derivative[i, m] = barycentric[m] / barycentric[i] / (points[i] - points[m])
    for i in range(4):
        derivative[i, i] = -np.sum(derivative[i])
    halves = []
    for h in range(2):
        shifted = (points + 2 * h - 1) / 2.0
        lagrange = np.ones((4, 4))
        for m in range(4):
            for k in range(4):
                if k != m:
                    lagrange[:, m] = (
                        lagrange[:, m] * (shifted - points[k]) / (points[m] - points[k])
                    )
        halves.append(lagrange)
    return derivative.astype(np.float32), np.stack(halves).astype(np.float32)


def split(value):
    high = value.astype(BF16)
    return high, (value - high.astype(F32)).astype(BF16)


def node_matrices():
    derivative, _ = node_tables()
    eye = np.eye(4, dtype=np.float32)
    slopes = [
        np.kron(np.kron(derivative.T, eye), eye),
        np.kron(np.kron(eye, derivative.T), eye),
        np.kron(np.kron(eye, eye), derivative.T),
    ]
    traces = []
    for node in (0, 3):
        traces.append(np.kron(np.kron(eye, eye[node : node + 1]), eye))
    for node in (0, 3):
        traces.append(np.kron(np.kron(eye, eye), eye[node : node + 1]))
    traces = np.concatenate(traces)
    rows = np.concatenate(slopes + [traces])
    high = rows.astype(ml_dtypes.bfloat16)
    low = (rows - high.astype(np.float32)).astype(ml_dtypes.bfloat16)
    forward = np.concatenate([high, high, low, low], axis=1)
    back = np.concatenate([traces.T, traces.T], axis=1).astype(ml_dtypes.bfloat16)
    return forward, back


def small_solve(gram):
    size = KRYLOV + 1
    norm = jnp.sqrt(gram[0][0] + 1e-6)
    one = jnp.ones_like(norm)
    basis = [[one / norm]]
    images = [[gram[0][i] / norm for i in range(size)]]
    hess = [[None] * KRYLOV for _ in range(size)]
    for column in range(KRYLOV):
        current = basis[column]
        mapped = [SHIFT * c for c in current] + [None]
        for i, c in enumerate(current):
            mapped[i + 1] = c if mapped[i + 1] is None else mapped[i + 1] + c
        for earlier in range(column + 1):
            product = sum(m * images[earlier][i] for i, m in enumerate(mapped))
            hess[earlier][column] = product
            for i, c in enumerate(basis[earlier]):
                mapped[i] = mapped[i] - product * c
        image = [sum(m * gram[k][i] for k, m in enumerate(mapped)) for i in range(size)]
        square = sum(m * image[i] for i, m in enumerate(mapped))
        length = jnp.sqrt(jnp.maximum(square, 0.0) + 1e-6)
        hess[column + 1][column] = length
        if column + 1 < KRYLOV:
            scale = one / length
            basis.append([m * scale for m in mapped])
            images.append([m * scale for m in image])
    normal = [[None] * KRYLOV for _ in range(KRYLOV)]
    for i in range(KRYLOV):
        for j in range(i + 1):
            normal[i][j] = sum(hess[r][i] * hess[r][j] for r in range(j + 2))
    factor = [[None] * KRYLOV for _ in range(KRYLOV)]
    inverse = [None] * KRYLOV
    for j in range(KRYLOV):
        pivot = normal[j][j]
        for k in range(j):
            pivot = pivot - factor[j][k] * factor[j][k]
        factor[j][j] = jnp.sqrt(pivot)
        inverse[j] = one / factor[j][j]
        for i in range(j + 1, KRYLOV):
            value = normal[i][j]
            for k in range(j):
                value = value - factor[i][k] * factor[j][k]
            factor[i][j] = value * inverse[j]
    half = []
    for i in range(KRYLOV):
        value = norm * hess[0][i]
        for k in range(i):
            value = value - factor[i][k] * half[k]
        half.append(value * inverse[i])
    weights = [None] * KRYLOV
    for i in reversed(range(KRYLOV)):
        value = half[i]
        for k in range(i + 1, KRYLOV):
            value = value - factor[k][i] * weights[k]
        weights[i] = value * inverse[i]
    return [
        sum(weights[j] * basis[j][i] for j in range(i, KRYLOV)) for i in range(KRYLOV)
    ]


def kernel(
    sizes,
    source,
    diagonal,
    volume,
    surface,
    pack,
    forward,
    back,
    out,
    xs,
    slopes,
    right,
    traces,
    halo_x,
    halo_y,
    halo_z,
    neighbour_pack,
    gather_left,
    pick_own,
    pick_halo,
    place,
    coupling,
    maps,
    rows,
    rows_left,
    faces,
    faces_left,
    gram,
    message,
    messages,
    send_sem,
    recv_sem,
    pack_send,
    pack_recv,
    sum_send,
    sum_recv,
):
    axes = ("gx", "gy", "gz")
    here = [lax.axis_index(a) for a in axes]
    group = sizes[0] * sizes[1] * sizes[2]
    me = (here[0] * sizes[1] + here[1]) * sizes[2] + here[2]
    has_low = [h > 0 for h in here]
    has_high = [h < n - 1 for h, n in zip(here, sizes)]

    def peer(step):
        other = lax.rem(me + step, group)
        return {
            "gx": other // (sizes[1] * sizes[2]),
            "gy": lax.rem(other // sizes[2], sizes[1]),
            "gz": lax.rem(other, sizes[2]),
        }

    barrier = pltpu.get_barrier_semaphore()

    @pl.loop(1, group)
    def _(step):
        pl.semaphore_signal(barrier, inc=1, device_id=peer(step), device_id_type=MESH)

    xs[0] = source[...]
    halos = (halo_x, halo_y, halo_z)
    for d in range(3):
        for s, there in ((0, has_low[d]), (1, has_high[d])):

            @pl.when(jnp.logical_not(there))
            def _(d=d, s=s):
                for k in range(KRYLOV):
                    halos[d][k, s] = jnp.zeros((5, 16, LANES), F32)

                if d == 0:
                    neighbour_pack[s] = jnp.full((32, LANES), -9.0, F32)

    pl.semaphore_wait(barrier, group - 1)

    def to(d, s):
        return {axes[d]: here[d] - 1 if s == 0 else here[d] + 1}

    def pack_copy(s):
        return pltpu.make_async_remote_copy(
            src_ref=pack,
            dst_ref=neighbour_pack.at[1 - s],
            send_sem=pack_send.at[s],
            recv_sem=pack_recv.at[s],
            device_id=to(0, s),
            device_id_type=MESH,
        )

    def face_copy(d, s, k):
        if d == 0:
            face = xs.at[k, :, pl.ds(48 * s, 16), :]
        else:
            face = traces.at[k, 2 * (d - 1) + s]
        return pltpu.make_async_remote_copy(
            src_ref=face,
            dst_ref=halos[d].at[k, 1 - s],
            send_sem=send_sem.at[k, d, s],
            recv_sem=recv_sem.at[k, d, s],
            device_id=to(d, s),
            device_id_type=MESH,
        )

    def sides(d, s):
        return (has_low[d], has_high[d]) if s == 0 else (has_high[d], has_low[d])

    def start(d, k):
        for s in range(2):
            target, _ = sides(d, s)

            @pl.when(target)
            def _(s=s):
                face_copy(d, s, k).start()

    def arrive(d, k):
        for s in range(2):
            target, origin = sides(d, s)

            @pl.when(origin)
            def _(s=s):
                face_copy(d, s, k).wait_recv()

            @pl.when(target)
            def _(s=s):
                face_copy(d, s, k).wait_send()

    for s in range(2):

        @pl.when(sides(0, s)[0])
        def _(s=s):
            pack_copy(s).start()

    lane = lax.broadcasted_iota(jnp.int32, (1, LANES), 1)
    left_half = lane < 64
    _, halves = node_tables()

    def keys(packed, me_x):
        offset = packed[25:26] - me_x
        fine, coarse, quarter, side = (packed[r : r + 1] for r in range(26, 30))
        odd = jnp.floor(side * 0.5)
        opposite = side + 1.0 - 2.0 * (side - 2.0 * odd)
        return offset, fine, coarse, quarter, side, opposite

    def one_hot(key, count):
        index = lax.broadcasted_iota(jnp.int32, (count, LANES), 0).astype(F32)
        return jnp.where(index == key, 1.0, 0.0).astype(BF16)

    def make_maps(slot, quarter, flipped):
        first = quarter >= 2.0
        second = (quarter - 2.0 * jnp.where(first, 1.0, 0.0)) >= 1.0
        for stage, bit in ((0, first), (1, second)):
            for i in range(4):
                for m in range(4):
                    straight = jnp.where(bit, float(halves[1, i, m]), float(halves[0, i, m]))
                    turned = jnp.where(bit, float(halves[1, m, i]), float(halves[0, m, i]))
                    row = 16 * stage + 4 * i + m
                    maps[slot, row : row + 1] = jnp.where(flipped, turned, straight)

    own = pack[...]
    place_x = here[0].astype(F32)
    offset, fine, coarse, quarter, side, opposite = keys(own, place_x)
    same = offset == 0.0
    at_coarse = jnp.where(same, opposite * LANES + coarse, -1.0)
    at_fine = side * LANES + fine
    pick_own[...] = one_hot(
        jnp.where(left_half, at_coarse, jnp.where(same, at_fine, -1.0)), 768
    )
    outside = jnp.where(offset < 0.0, coarse, LANES + coarse)
    pick_halo[:, 0:128] = one_hot(
        jnp.where(left_half & jnp.logical_not(same), outside, -1.0), 256
    )
    place[:, 0:128] = one_hot(jnp.where(left_half, at_fine, at_coarse), 768)
    coupling[0] = own
    make_maps(0, quarter, jnp.logical_not(left_half))

    def from_neighbours():
        for s in range(2):
            target, origin = sides(0, s)

            @pl.when(origin)
            def _(s=s):
                pack_copy(s).wait_recv()

            @pl.when(target)
            def _(s=s):
                pack_copy(s).wait_send()

        both = jnp.where(left_half, pltpu.roll(neighbour_pack[0], 64, 1), neighbour_pack[1])
        offset, fine, coarse, quarter, _, _ = keys(both, place_x)
        valid = offset == 0.0
        base = jnp.where(left_half, 0.0, 1.0 * LANES)
        pick_halo[:, 128:256] = one_hot(jnp.where(valid, base + fine, -1.0), 256)
        place[:, 128:256] = one_hot(jnp.where(valid, base + coarse, -1.0), 768)
        coupling[1] = jnp.where(valid, both, 0.0)
        make_maps(1, jnp.where(valid, quarter, 0.0), lane >= 0)

    def put_trace(block, var, value):
        high, low = split(value)
        columns = pl.ds(block * LANES, LANES)
        gather_left[pl.ds(16 * var, 16), columns] = high
        gather_left[pl.ds(80 + 16 * var, 16), columns] = low

    def products(k, count):
        @pl.loop(0, count)
        def _(i):
            total = jnp.zeros((8, LANES), F32)
            for b in range(5):
                both = xs[k, b] * xs[i, b]
                for r in range(8):
                    total = total + both[8 * r : 8 * r + 8]
            gram[pl.ds(k * 8 + i, 1), :] = jnp.sum(total, axis=0, keepdims=True)

    gram[...] = jnp.zeros_like(gram)

    @pl.loop(0, KRYLOV)
    def _(k):
        start(0, k)
        for b in range(5):
            high, low = split(xs[k, b])
            columns = slice(b * LANES, (b + 1) * LANES)
            right[0:64, columns] = high
            right[64:128, columns] = low
            right[128:192, columns] = high
            right[192:256, columns] = low
        slopes[...] = jnp.dot(forward[...], right[...], preferred_element_type=F32)
        for f in range(4):
            for b in range(5):
                traces[k, f, b] = slopes[
                    192 + 16 * f : 208 + 16 * f, b * LANES : (b + 1) * LANES
                ]
        start(1, k)
        start(2, k)

        @pl.when(k == 0)
        def _():
            from_neighbours()

        for b in range(5):
            put_trace(0, b, xs[k, b, 0:16])
            put_trace(1, b, xs[k, b, 48:64])
            for f in range(4):
                put_trace(2 + f, b, traces[k, f, b])
        gathered = jnp.dot(
            gather_left[:, 0:768], pick_own[...], preferred_element_type=F32
        )
        rows[0] = gathered[0:80] + gathered[80:160]

        @pl.loop(0, 4)
        def _(c):
            chunk = pl.ds(pl.multiple_of(16 * c, 16), 16)
            total = [
                (diagonal[a, chunk].astype(F32) - SHIFT) * xs[k, a, chunk] for a in range(5)
            ]
            for d in range(3):
                for b in range(5):
                    slope = slopes[
                        pl.ds(pl.multiple_of(64 * d + 16 * c, 16), 16),
                        b * LANES : (b + 1) * LANES,
                    ]
                    for a in range(5):
                        total[a] = total[a] + volume[d, a, b, chunk].astype(F32) * slope
            for a in range(5):
                xs[k + 1, a, chunk] = total[a]

        products(k, k + 1)
        arrive(0, k)
        arrive(1, k)
        arrive(2, k)
        for s in range(2):
            for b in range(5):
                put_trace(6 + s, b, halo_x[k, s, b])
        gathered = jnp.dot(
            gather_left[:, 768:1024], pick_halo[...], preferred_element_type=F32
        )
        gathered = gathered[0:80] + gathered[80:160]
        rows[0] = rows[0] + gathered[:, 0:128]
        rows[1] = gathered[:, 128:256]
        for g in range(2):
            before = [rows[g, 16 * b : 16 * b + 16] for b in range(5)]
            for a in range(5):
                value = coupling[g, 5 * a : 5 * a + 1] * before[0]
                for b in range(1, 5):
                    row = 5 * a + b
                    value = value + coupling[g, row : row + 1] * before[b]
                rows[g, 16 * a : 16 * a + 16] = value
            nodes = [rows[g, pl.ds(m, 5, stride=16), :] for m in range(16)]
            for stage in range(2):
                after = [None] * 16
                for i in range(4):
                    for j in range(4):
                        own_index = i if stage == 0 else j
                        for m in range(4):
                            row = 16 * stage + 4 * own_index + m
                            node = 4 * m + j if stage == 0 else 4 * i + m
                            term = maps[g, row : row + 1] * nodes[node]
                            at = 4 * i + j
                            after[at] = term if m == 0 else after[at] + term
                nodes = after
            for m in range(16):
                rows[g, pl.ds(m, 5, stride=16), :] = nodes[m]
            high, low = split(rows[g])
            rows_left[0:80, g * LANES : (g + 1) * LANES] = high
            rows_left[80:160, g * LANES : (g + 1) * LANES] = low
        faces[...] = lax.dot_general(
            rows_left[...], place[...], (((1,), (1,)), ((), ())), preferred_element_type=F32
        )
        for f in range(6):
            d, s = f // 2, f % 2
            if d == 0:
                beside = [halo_x[k, s, b] for b in range(5)]
            elif d == 1:
                beside = [halo_y[k, s, b] for b in range(5)]
            else:
                edge = lane == (LANES - 1 if s == 0 else 0)
                turn = 1 if s == 0 else LANES - 1
                beside = [
                    pltpu.roll(
                        jnp.where(edge, halo_z[k, s, b], traces[k, 3 - s, b]), turn, 1
                    )
                    for b in range(5)
                ]
            columns = slice(f * LANES, (f + 1) * LANES)
            for a in range(5):
                value = (
                    faces[16 * a : 16 * a + 16, columns]
                    + faces[80 + 16 * a : 96 + 16 * a, columns]
                )
                for b in range(5):
                    value = value + surface[f, a, b].astype(F32) * beside[b]
                if d == 0:
                    at = 48 * s
                    xs[k + 1, a, at : at + 16] = xs[k + 1, a, at : at + 16] + value
                else:
                    high, low = split(value)
                    at = 16 * (f - 2)
                    faces_left[at : at + 16, a * LANES : (a + 1) * LANES] = high
                    faces_left[64 + at : 80 + at, a * LANES : (a + 1) * LANES] = low
        added = jnp.dot(back[...], faces_left[...], preferred_element_type=F32)
        for a in range(5):
            xs[k + 1, a] = xs[k + 1, a] + added[:, a * LANES : (a + 1) * LANES]

    products(KRYLOV, KRYLOV + 1)
    message[...] = lax.dot_general(
        jnp.ones((8, LANES), F32),
        gram[...],
        (((1,), (1,)), ((), ())),
        preferred_element_type=F32,
        precision=lax.Precision.HIGHEST,
    )

    def sum_copy(step):
        return pltpu.make_async_remote_copy(
            src_ref=message,
            dst_ref=messages.at[step],
            send_sem=sum_send.at[step],
            recv_sem=sum_recv.at[step],
            device_id=peer(step),
            device_id_type=MESH,
        )

    @pl.loop(1, group)
    def _(step):
        sum_copy(step).start()

    messages[0] = message[...]

    @pl.loop(1, group)
    def _(step):
        sum_copy(step).wait_recv()

    @pl.loop(1, group)
    def _(step):
        sum_copy(step).wait_send()

    def add(i, total):
        return total + messages[lax.rem(i + group - me, group)]

    total = lax.fori_loop(0, group, add, jnp.zeros((8, LANES), F32))
    size = KRYLOV + 1
    entries = [[None] * size for _ in range(size)]
    for k in range(size):
        for i in range(k + 1):
            entry = jnp.sum(jnp.where(lane == 8 * k + i, total, 0.0), axis=1, keepdims=True)
            entry = jnp.broadcast_to(entry, (8, LANES))
            entries[k][i] = entries[i][k] = entry
    scales = small_solve(entries)
    for b in range(5):
        for r in range(8):
            at = slice(8 * r, 8 * r + 8)
            value = scales[0] * xs[0, b, at]
            for k in range(1, KRYLOV):
                value = value + scales[k] * xs[k, b, at]
            out[b, at] = value


def local(
    sizes,
    adjoint_source,
    diagonal,
    volume_coupling,
    surface_coupling,
    mortar_owner,
    mortar_fine,
    mortar_coarse,
    mortar_quarter,
    mortar_side,
    mortar_coupling,
):
    forward, back = node_matrices()
    count = mortar_fine.shape[0]
    numbers = jnp.stack(
        [mortar_owner[:, 0], mortar_fine, mortar_coarse, mortar_quarter, mortar_side]
    ).astype(F32)
    pairs = mortar_coupling.reshape(count, 2, 25).transpose(2, 1, 0).reshape(25, 2 * count)
    pack = jnp.concatenate(
        [pairs, jnp.concatenate([numbers, numbers], axis=1), jnp.zeros((2, 2 * count), F32)]
    )
    group = sizes[0] * sizes[1] * sizes[2]
    vmem = pl.BlockSpec(memory_space=pltpu.VMEM)
    dma = pltpu.SemaphoreType.DMA
    result = pl.pallas_call(
        functools.partial(kernel, sizes),
        out_shape=jax.ShapeDtypeStruct((5, 64, LANES), F32),
        in_specs=[vmem] * 7,
        out_specs=vmem,
        scratch_shapes=[
            pltpu.VMEM((KRYLOV + 1, 5, 64, LANES), F32),
            pltpu.VMEM((256, 5 * LANES), F32),
            pltpu.VMEM((256, 5 * LANES), BF16),
            pltpu.VMEM((KRYLOV, 4, 5, 16, LANES), F32),
            pltpu.VMEM((KRYLOV, 2, 5, 16, LANES), F32),
            pltpu.VMEM((KRYLOV, 2, 5, 16, LANES), F32),
            pltpu.VMEM((KRYLOV, 2, 5, 16, LANES), F32),
            pltpu.VMEM((2, 32, LANES), F32),
            pltpu.VMEM((160, 8 * LANES), BF16),
            pltpu.VMEM((6 * LANES, LANES), BF16),
            pltpu.VMEM((2 * LANES, 2 * LANES), BF16),
            pltpu.VMEM((6 * LANES, 2 * LANES), BF16),
            pltpu.VMEM((2, 32, LANES), F32),
            pltpu.VMEM((2, 32, LANES), F32),
            pltpu.VMEM((2, 80, LANES), F32),
            pltpu.VMEM((160, 2 * LANES), BF16),
            pltpu.VMEM((160, 6 * LANES), F32),
            pltpu.VMEM((128, 5 * LANES), BF16),
            pltpu.VMEM((LANES, LANES), F32),
            pltpu.VMEM((8, LANES), F32),
            pltpu.VMEM((group, 8, LANES), F32),
            dma((KRYLOV, 3, 2)),
            dma((KRYLOV, 3, 2)),
            dma((2,)),
            dma((2,)),
            dma((group,)),
            dma((group,)),
        ],
        compiler_params=pltpu.CompilerParams(
            collective_id=0, has_side_effects=True, vmem_limit_bytes=48 * 1024 * 1024
        ),
    )(
        adjoint_source.reshape(5, 64, LANES),
        diagonal.reshape(5, 64, LANES),
        volume_coupling.reshape(3, 5, 5, 64, LANES),
        surface_coupling.reshape(6, 5, 5, 16, LANES),
        pack,
        jnp.asarray(forward),
        jnp.asarray(back),
    )
    return result.reshape(adjoint_source.shape)


def solution(mesh):
    placed = (
        P(None, None, None, None, ("groups", "gx"), "gy", "gz"),
        P(None, None, None, None, ("groups", "gx"), "gy", "gz"),
        P(None, None, None, None, None, None, ("groups", "gx"), "gy", "gz"),
        P(None, None, None, None, None, ("groups", "gx"), "gy", "gz"),
        P(("groups", "gx", "gy", "gz"), None),
        P(("groups", "gx", "gy", "gz")),
        P(("groups", "gx", "gy", "gz")),
        P(("groups", "gx", "gy", "gz")),
        P(("groups", "gx", "gy", "gz")),
        P(("groups", "gx", "gy", "gz"), None, None, None),
    )
    sizes = tuple(mesh.shape[a] for a in ("gx", "gy", "gz"))
    return jax.shard_map(
        functools.partial(local, sizes),
        mesh=mesh,
        in_specs=placed,
        out_specs=P(None, None, None, None, ("groups", "gx"), "gy", "gz"),
        check_vma=False,
    )
```

profile of v0, /device:TPU:0, one launch (start us, length us, event | category | flops | bytes accessed | tf_op | source)
XLA Modules:
  0.0 36.0 jit_solution(6898052337239907748)
XLA Ops:
  0.0 0.1 pad.3.clone
  0.1 0.7 %stack.19 = s32[5,64]{1,0:T(8,128)S(1)} concatenate(s32[1,64]{1,0:T(1,128)} %bitcast.21, s32[1,64]{1,0:T(1,128)} %bitcast.22, s32[1,64]{1,0:T(1,128)} %bitcast.23, s32[1,64]{1,0:T(1,128)} %bitcast.24, s32[1,64]{1,0:T(1,128)} %bitcast.25), dimensions={0} | concatenate | bytes 2560 | tf_op jit(solution)/shard_map/stack | solution.py:540
  0.8 0.8 %reshape.26 = f32[25,128]{1,0:T(8,128)S(1)} reshape(f32[25,2,64]{2,1,0:T(2,128)} %bitcast.20) | data formatting | bytes 25600 | tf_op jit(solution)/shard_map/reshape | solution.py:543
  1.6 0.1 maximum_maximum_fusion.pack
  1.7 0.0 copy-start
  1.7 1.3 %copy-done = bf16[3,5,5,4,4,4,1,1,128]{8,5,7,6,4,3,2,1,0:T(4,128)(2,1)S(1)} copy-done((bf16[3,5,5,4,4,4,1,1,128]{8,5,7,6,4,3,2,1,0:T(4,128)(2,1)S(1)}, bf16[3,5,5,4,4,4,1,1,128]{8,5,7,6,4,3,2,1,0:T(4,128)(2,1)}, u32[]{:S(2)}) %copy-start) | copy-done | bytes 1228824
  3.0 0.0 copy-start.1
  3.0 1.1 %copy-done.1 = bf16[6,5,5,4,4,1,1,128]{7,4,6,5,3,2,1,0:T(4,128)(2,1)S(1)} copy-done((bf16[6,5,5,4,4,1,1,128]{7,4,6,5,3,2,1,0:T(4,128)(2,1)S(1)}, bf16[6,5,5,4,4,1,1,128]{7,4,6,5,3,2,1,0:T(4,128)(2,1)}, u32[]{:S(2)}) %copy-start.1) | copy-done | bytes 614424
  4.1 0.0 copy-start.2
  4.1 0.9 %copy-done.2 = f32[5,4,4,4,1,1,128]{6,5,4,3,2,1,0:T(1,128)S(1)} copy-done((f32[5,4,4,4,1,1,128]{6,5,4,3,2,1,0:T(1,128)S(1)}, f32[5,4,4,4,1,1,128]{6,5,4,3,2,1,0:T(1,128)}, u32[]{:S(2)}) %copy-start.2) | copy-done | bytes 163864
  5.0 0.0 copy-start.3
  5.0 0.9 %copy-done.3 = bf16[256,256]{1,0:T(8,128)(2,1)S(1)} copy-done((bf16[256,256]{1,0:T(8,128)(2,1)S(1)}, bf16[256,256]{1,0:T(8,128)(2,1)}, u32[]{:S(2)}) %copy-start.3) | copy-done | bytes 131096
  5.9 0.0 copy-start.4
  5.9 0.9 %copy-done.4 = bf16[5,4,4,4,1,1,128]{6,3,5,4,2,1,0:T(4,128)(2,1)S(1)} copy-done((bf16[5,4,4,4,1,1,128]{6,3,5,4,2,1,0:T(4,128)(2,1)S(1)}, bf16[5,4,4,4,1,1,128]{6,3,5,4,2,1,0:T(4,128)(2,1)}, u32[]{:S(2)}) %copy-start.4) | copy-done | bytes 81944
  6.8 0.0 copy-start.5
  6.8 0.7 %copy-done.5 = bf16[64,128]{1,0:T(8,128)(2,1)S(1)} copy-done((bf16[64,128]{1,0:T(8,128)(2,1)S(1)}, bf16[64,128]{1,0:T(8,128)(2,1)}, u32[]{:S(2)}) %copy-start.5) | copy-done | bytes 16408
  7.5 27.8 %shard_map.118 = f32[5,64,128]{2,1,0:T(8,128)S(1)} custom-call(f32[5,64,128]{2,1,0:T(8,128)S(1)} %bitcast.18, bf16[5,64,128]{2,1,0:T(8,128)(2,1)S(1)} %bitcast.19, bf16[3,5,5,64,128]{4,3,2,1,0:T(8,128)(2,1)S(1)} %bitcast.15, bf16[6,5,5,16,128]{4,3,2,1,0:T(8,128)(2,1)S(1)} %bitcast.17, f32[32,128]{1,0:T(8,128)S(1)} %maximum_maximum_fusion.pack, ...), custom_call_target="tpu_custom_call" | custom-call | tf_op jit(solution)/shard_map/pallas_call | solution.py:550
  35.3 0.7 %copy.15 = f32[5,4,4,4,1,1,128]{6,5,4,3,2,1,0:T(1,128)} copy(f32[5,4,4,4,1,1,128]{6,5,4,3,2,1,0:T(1,128)S(1)} %bitcast.16) | data formatting | bytes 327680
  (2 shorter events, 0.0 us)
Async XLA Ops:
  1.7 1.3 %copy-start = (bf16[3,5,5,4,4,4,1,1,128]{8,5,7,6,4,3,2,1,0:T(4,128)(2,1)S(1)}, bf16[3,5,5,4,4,4,1,1,128]{8,5,7,6,4,3,2,1,0:T(4,128)(2,1)}, u32[]{:S(2)}) copy-start(bf16[3,5,5,4,4,4,1,1,128]{8,5,7,6,4,3,2,1,0:T(4,128)(2,1)} %param.14) | copy-start | bytes 3686404
  3.0 1.1 %copy-start.1 = (bf16[6,5,5,4,4,1,1,128]{7,4,6,5,3,2,1,0:T(4,128)(2,1)S(1)}, bf16[6,5,5,4,4,1,1,128]{7,4,6,5,3,2,1,0:T(4,128)(2,1)}, u32[]{:S(2)}) copy-start(bf16[6,5,5,4,4,1,1,128]{7,4,6,5,3,2,1,0:T(4,128)(2,1)} %param.15) | copy-start | bytes 1843204
  4.1 0.9 %copy-start.2 = (f32[5,4,4,4,1,1,128]{6,5,4,3,2,1,0:T(1,128)S(1)}, f32[5,4,4,4,1,1,128]{6,5,4,3,2,1,0:T(1,128)}, u32[]{:S(2)}) copy-start(f32[5,4,4,4,1,1,128]{6,5,4,3,2,1,0:T(1,128)} %param.12) | copy-start | bytes 491524
  5.0 0.9 %copy-start.3 = (bf16[256,256]{1,0:T(8,128)(2,1)S(1)}, bf16[256,256]{1,0:T(8,128)(2,1)}, u32[]{:S(2)}) copy-start(bf16[256,256]{1,0:T(8,128)(2,1)} %constant.6.clone.forward) | copy-start | bytes 393220
  5.9 0.9 %copy-start.4 = (bf16[5,4,4,4,1,1,128]{6,3,5,4,2,1,0:T(4,128)(2,1)S(1)}, bf16[5,4,4,4,1,1,128]{6,3,5,4,2,1,0:T(4,128)(2,1)}, u32[]{:S(2)}) copy-start(bf16[5,4,4,4,1,1,128]{6,3,5,4,2,1,0:T(4,128)(2,1)} %param.13) | copy-start | bytes 245764
  6.8 0.7 %copy-start.5 = (bf16[64,128]{1,0:T(8,128)(2,1)S(1)}, bf16[64,128]{1,0:T(8,128)(2,1)}, u32[]{:S(2)}) copy-start(bf16[64,128]{1,0:T(8,128)(2,1)} %constant.7.clone.back) | copy-start | bytes 49156
where the time goes:
time: 36.4 us; the launch traced here: 36 us
  Pallas kernels  27.8 us (76%)
  local copies, waits for them, and re-layouts  8.09 us (22%)
    pallas_call x1, Pallas kernels, local(): pl.pallas_call(functools.partial(kernel, sizes), out_shape=jax.ShapeDtype...  27.8 us
    unnamed x13, local copies, waits for them, and re-layouts  6.45 us
    reshape x1, local copies, waits for them, and re-layouts, local(): mortar_coupling.reshape(count, 2, 25).transpose(2, 1, 0)  0.82 us
    another operation x1, local copies, waits for them, and re-layouts, local(): jnp.stack([mortar_owner[:, 0], mortar_fine, mortar_coarse, mortar_quarter...  0.74 us

commit v1 on v0

--- a/solution.py
+++ b/solution.py
@@ -131,14 +131,28 @@
 
 def kernel(
     sizes,
-    source,
+    source_hbm,
+    diagonal_hbm,
+    volume_hbm,
+    surface_hbm,
+    owner_hbm,
+    fine_hbm,
+    coarse_hbm,
+    quarter_hbm,
+    side_hbm,
+    coupling_hbm,
+    forward_hbm,
+    back_hbm,
+    out,
     diagonal,
     volume,
     surface,
-    pack,
+    numbers,
+    pairs,
     forward,
     back,
-    out,
+    pack,
+    load_sem,
     xs,
     slopes,
     right,
@@ -182,13 +196,33 @@
             "gz": lax.rem(other, sizes[2]),
         }
 
+    loads = [
+        pltpu.make_async_copy(origin, target, load_sem.at[i])
+        for i, (origin, target) in enumerate(
+            (
+                (source_hbm, xs.at[0]),
+                (owner_hbm, numbers.at[0]),
+                (fine_hbm, numbers.at[1]),
+                (coarse_hbm, numbers.at[2]),
+                (quarter_hbm, numbers.at[3]),
+                (side_hbm, numbers.at[4]),
+                (coupling_hbm, pairs),
+                (forward_hbm, forward),
+                (diagonal_hbm, diagonal),
+                (volume_hbm, volume),
+                (surface_hbm, surface),
+                (back_hbm, back),
+            )
+        )
+    ]
+    for load in loads:
+        load.start()
     barrier = pltpu.get_barrier_semaphore()
 
     @pl.loop(1, group)
     def _(step):
         pl.semaphore_signal(barrier, inc=1, device_id=peer(step), device_id_type=MESH)
 
-    xs[0] = source[...]
     halos = (halo_x, halo_y, halo_z)
     for d in range(3):
         for s, there in ((0, has_low[d]), (1, has_high[d])):
@@ -201,6 +235,14 @@
                 if d == 0:
                     neighbour_pack[s] = jnp.full((32, LANES), -9.0, F32)
 
+    for load in loads[1:7]:
+        load.wait()
+    for half in range(2):
+        at = slice(64 * half, 64 * half + 64)
+        pack[0:25, at] = pairs[:, half, :]
+        for i in range(5):
+            pack[25 + i : 26 + i, at] = numbers[i].astype(F32)
+    pack[30:32] = jnp.zeros((2, LANES), F32)
     pl.semaphore_wait(barrier, group - 1)
 
     def to(d, s):
@@ -285,22 +327,24 @@
                     row = 16 * stage + 4 * i + m
                     maps[slot, row : row + 1] = jnp.where(flipped, turned, straight)
 
-    own = pack[...]
     place_x = here[0].astype(F32)
-    offset, fine, coarse, quarter, side, opposite = keys(own, place_x)
-    same = offset == 0.0
-    at_coarse = jnp.where(same, opposite * LANES + coarse, -1.0)
-    at_fine = side * LANES + fine
-    pick_own[...] = one_hot(
-        jnp.where(left_half, at_coarse, jnp.where(same, at_fine, -1.0)), 768
-    )
-    outside = jnp.where(offset < 0.0, coarse, LANES + coarse)
-    pick_halo[:, 0:128] = one_hot(
-        jnp.where(left_half & jnp.logical_not(same), outside, -1.0), 256
-    )
-    place[:, 0:128] = one_hot(jnp.where(left_half, at_fine, at_coarse), 768)
-    coupling[0] = own
-    make_maps(0, quarter, jnp.logical_not(left_half))
+
+    def from_own():
+        own = pack[...]
+        offset, fine, coarse, quarter, side, opposite = keys(own, place_x)
+        same = offset == 0.0
+        at_coarse = jnp.where(same, opposite * LANES + coarse, -1.0)
+        at_fine = side * LANES + fine
+        pick_own[...] = one_hot(
+            jnp.where(left_half, at_coarse, jnp.where(same, at_fine, -1.0)), 768
+        )
+        outside = jnp.where(offset < 0.0, coarse, LANES + coarse)
+        pick_halo[:, 0:128] = one_hot(
+            jnp.where(left_half & jnp.logical_not(same), outside, -1.0), 256
+        )
+        place[:, 0:128] = one_hot(jnp.where(left_half, at_fine, at_coarse), 768)
+        coupling[0] = own
+        make_maps(0, quarter, jnp.logical_not(left_half))
 
     def from_neighbours():
         for s in range(2):
@@ -340,6 +384,7 @@
             gram[pl.ds(k * 8 + i, 1), :] = jnp.sum(total, axis=0, keepdims=True)
 
     gram[...] = jnp.zeros_like(gram)
+    loads[0].wait()
 
     @pl.loop(0, KRYLOV)
     def _(k):
@@ -351,6 +396,11 @@
             right[64:128, columns] = low
             right[128:192, columns] = high
             right[192:256, columns] = low
+
+        @pl.when(k == 0)
+        def _():
+            loads[7].wait()
+
         slopes[...] = jnp.dot(forward[...], right[...], preferred_element_type=F32)
         for f in range(4):
             for b in range(5):
@@ -362,7 +412,9 @@
 
         @pl.when(k == 0)
         def _():
-            from_neighbours()
+            from_own()
+            loads[8].wait()
+            loads[9].wait()
 
         for b in range(5):
             put_trace(0, b, xs[k, b, 0:16])
@@ -395,6 +447,13 @@
         arrive(0, k)
         arrive(1, k)
         arrive(2, k)
+
+        @pl.when(k == 0)
+        def _():
+            from_neighbours()
+            loads[10].wait()
+            loads[11].wait()
+
         for s in range(2):
             for b in range(5):
                 put_trace(6 + s, b, halo_x[k, s, b])
@@ -537,22 +596,25 @@
 ):
     forward, back = node_matrices()
     count = mortar_fine.shape[0]
-    numbers = jnp.stack(
-        [mortar_owner[:, 0], mortar_fine, mortar_coarse, mortar_quarter, mortar_side]
-    ).astype(F32)
-    pairs = mortar_coupling.reshape(count, 2, 25).transpose(2, 1, 0).reshape(25, 2 * count)
-    pack = jnp.concatenate(
-        [pairs, jnp.concatenate([numbers, numbers], axis=1), jnp.zeros((2, 2 * count), F32)]
-    )
+    pairs = mortar_coupling.transpose(2, 3, 1, 0).reshape(25, 2, count)
     group = sizes[0] * sizes[1] * sizes[2]
     vmem = pl.BlockSpec(memory_space=pltpu.VMEM)
     dma = pltpu.SemaphoreType.DMA
     result = pl.pallas_call(
         functools.partial(kernel, sizes),
         out_shape=jax.ShapeDtypeStruct((5, 64, LANES), F32),
-        in_specs=[vmem] * 7,
+        in_specs=[pl.BlockSpec(memory_space=pltpu.HBM)] * 12,
         out_specs=vmem,
         scratch_shapes=[
+            pltpu.VMEM((5, 64, LANES), BF16),
+            pltpu.VMEM((3, 5, 5, 64, LANES), BF16),
+            pltpu.VMEM((6, 5, 5, 16, LANES), BF16),
+            pltpu.VMEM((5, 1, 64), jnp.int32),
+            pltpu.VMEM((25, 2, 64), F32),
+            pltpu.VMEM((256, 256), BF16),
+            pltpu.VMEM((64, 128), BF16),
+            pltpu.VMEM((32, LANES), F32),
+            dma((12,)),
             pltpu.VMEM((KRYLOV + 1, 5, 64, LANES), F32),
             pltpu.VMEM((256, 5 * LANES), F32),
             pltpu.VMEM((256, 5 * LANES), BF16),
@@ -582,14 +644,19 @@
             dma((group,)),
         ],
         compiler_params=pltpu.CompilerParams(
-            collective_id=0, has_side_effects=True, vmem_limit_bytes=48 * 1024 * 1024
+            collective_id=0, has_side_effects=True, vmem_limit_bytes=63 * 1024 * 1024
         ),
     )(
         adjoint_source.reshape(5, 64, LANES),
         diagonal.reshape(5, 64, LANES),
         volume_coupling.reshape(3, 5, 5, 64, LANES),
         surface_coupling.reshape(6, 5, 5, 16, LANES),
-        pack,
+        mortar_owner.reshape(1, count),
+        mortar_fine.reshape(1, count),
+        mortar_coarse.reshape(1, count),
+        mortar_quarter.reshape(1, count),
+        mortar_side.reshape(1, count),
+        pairs,
         jnp.asarray(forward),
         jnp.asarray(back),
     )

time: 36.4 us -> 30.2 us (0.83)
  local copies, waits for them, and re-layouts: 8.09 us -> 1.59 us
  Pallas kernels: 27.8 us -> 28.5 us
    unnamed x13 -> x1, local copies, waits for them, and re-layouts: 6.45 us -> 1.59 us
    reshape x1 -> x0, local copies, waits for them, and re-layouts: 0.82 us -> none  [local(): mortar_coupling.reshape(count, 2, 25).transpose(2, 1, 0)]
    another operation x1 -> x0, local copies, waits for them, and re-layouts: 0.74 us -> none  [local(): jnp.stack([mortar_owner[:, 0], mortar_fine, mortar_coarse, mortar_quarter...]
    pallas_call x1, Pallas kernels: 27.8 us -> 28.5 us  [local(): pl.pallas_call(functools.partial(kernel, sizes), out_shape=jax.ShapeDtype...]
where the time goes in v1:
time: 30.2 us; the launch traced here: 30.1 us
  Pallas kernels  28.5 us (94%)
  local copies, waits for them, and re-layouts  1.59 us (5%)
    pallas_call x1, Pallas kernels, local(): pl.pallas_call(functools.partial(kernel, sizes), out_shape=jax.ShapeDtype...  28.5 us
    unnamed x1, local copies, waits for them, and re-layouts  1.59 us

profile of v1, /device:TPU:0, one launch (start us, length us, event | category | flops | bytes accessed | tf_op | source)
XLA Modules:
  0.0 30.1 jit_solution(11939579890414094397)
XLA Ops:
  0.0 28.5 %shard_map.118 = f32[5,64,128]{2,1,0:T(8,128)} custom-call(f32[5,64,128]{2,1,0:T(8,128)} %bitcast.18, bf16[5,64,128]{2,1,0:T(8,128)(2,1)} %bitcast.19, bf16[3,5,5,64,128]{4,3,2,1,0:T(8,128)(2,1)} %bitcast.15, bf16[6,5,5,16,128]{4,3,2,1,0:T(8,128)(2,1)} %bitcast.17, s32[1,64]{1,0:T(1,128)} %bitcast.21, s32[1,64]{1,0:T(1,128)} %bitcast.22, s32[1,64]{1,0:T(1,128)} %bitcast.23, ...), custom_call_target="tpu_custom_call" | custom-call | tf_op jit(solution)/shard_map/pallas_call | solution.py:603
  28.5 1.6 %copy.15 = f32[5,4,4,4,1,1,128]{6,5,4,3,2,1,0:T(1,128)} copy(f32[5,4,4,4,1,1,128]{6,5,4,3,2,1,0:T(1,128)} %bitcast.16) | data formatting | bytes 327680

commit v2 on v1

--- a/solution.py
+++ b/solution.py
@@ -62,7 +62,7 @@
     for node in (0, 3):
         traces.append(np.kron(np.kron(eye, eye), eye[node : node + 1]))
     traces = np.concatenate(traces)
-    rows = np.concatenate(slopes + [traces])
+    rows = np.concatenate(slopes)
     high = rows.astype(ml_dtypes.bfloat16)
     low = (rows - high.astype(np.float32)).astype(ml_dtypes.bfloat16)
     forward = np.concatenate([high, high, low, low], axis=1)
@@ -196,6 +196,12 @@
             "gz": lax.rem(other, sizes[2]),
         }
 
+    barrier = pltpu.get_barrier_semaphore()
+
+    @pl.loop(1, group)
+    def _(step):
+        pl.semaphore_signal(barrier, inc=1, device_id=peer(step), device_id_type=MESH)
+
     loads = [
         pltpu.make_async_copy(origin, target, load_sem.at[i])
         for i, (origin, target) in enumerate(
@@ -217,11 +223,6 @@
     ]
     for load in loads:
         load.start()
-    barrier = pltpu.get_barrier_semaphore()
-
-    @pl.loop(1, group)
-    def _(step):
-        pl.semaphore_signal(barrier, inc=1, device_id=peer(step), device_id_type=MESH)
 
     halos = (halo_x, halo_y, halo_z)
     for d in range(3):
@@ -389,6 +390,16 @@
     @pl.loop(0, KRYLOV)
     def _(k):
         start(0, k)
+        for s in range(2):
+            for b in range(5):
+                for i in range(4):
+                    at = 16 * i + 12 * s
+                    traces[k, s, b, 4 * i : 4 * i + 4] = xs[k, b, at : at + 4]
+        start(1, k)
+        for s in range(2):
+            for b in range(5):
+                traces[k, 2 + s, b] = xs[k, b, pl.ds(3 * s, 16, stride=4), :]
+        start(2, k)
         for b in range(5):
             high, low = split(xs[k, b])
             columns = slice(b * LANES, (b + 1) * LANES)
@@ -402,13 +413,6 @@
             loads[7].wait()
 
         slopes[...] = jnp.dot(forward[...], right[...], preferred_element_type=F32)
-        for f in range(4):
-            for b in range(5):
-                traces[k, f, b] = slopes[
-                    192 + 16 * f : 208 + 16 * f, b * LANES : (b + 1) * LANES
-                ]
-        start(1, k)
-        start(2, k)
 
         @pl.when(k == 0)
         def _():
@@ -444,9 +448,6 @@
                 xs[k + 1, a, chunk] = total[a]
 
         products(k, k + 1)
-        arrive(0, k)
-        arrive(1, k)
-        arrive(2, k)
 
         @pl.when(k == 0)
         def _():
@@ -454,6 +455,9 @@
             loads[10].wait()
             loads[11].wait()
 
+        arrive(0, k)
+        arrive(1, k)
+        arrive(2, k)
         for s in range(2):
             for b in range(5):
                 put_trace(6 + s, b, halo_x[k, s, b])
@@ -528,13 +532,14 @@
             xs[k + 1, a] = xs[k + 1, a] + added[:, a * LANES : (a + 1) * LANES]
 
     products(KRYLOV, KRYLOV + 1)
-    message[...] = lax.dot_general(
+    sums = lax.dot_general(
         jnp.ones((8, LANES), F32),
         gram[...],
         (((1,), (1,)), ((), ())),
         preferred_element_type=F32,
         precision=lax.Precision.HIGHEST,
     )
+    message[...] = sums[0:1]
 
     def sum_copy(step):
         return pltpu.make_async_remote_copy(
@@ -563,7 +568,7 @@
     def add(i, total):
         return total + messages[lax.rem(i + group - me, group)]
 
-    total = lax.fori_loop(0, group, add, jnp.zeros((8, LANES), F32))
+    total = lax.fori_loop(0, group, add, jnp.zeros((1, LANES), F32))
     size = KRYLOV + 1
     entries = [[None] * size for _ in range(size)]
     for k in range(size):
@@ -611,12 +616,12 @@
             pltpu.VMEM((6, 5, 5, 16, LANES), BF16),
             pltpu.VMEM((5, 1, 64), jnp.int32),
             pltpu.VMEM((25, 2, 64), F32),
-            pltpu.VMEM((256, 256), BF16),
+            pltpu.VMEM((192, 256), BF16),
             pltpu.VMEM((64, 128), BF16),
             pltpu.VMEM((32, LANES), F32),
             dma((12,)),
             pltpu.VMEM((KRYLOV + 1, 5, 64, LANES), F32),
-            pltpu.VMEM((256, 5 * LANES), F32),
+            pltpu.VMEM((192, 5 * LANES), F32),
             pltpu.VMEM((256, 5 * LANES), BF16),
             pltpu.VMEM((KRYLOV, 4, 5, 16, LANES), F32),
             pltpu.VMEM((KRYLOV, 2, 5, 16, LANES), F32),
@@ -634,8 +639,8 @@
             pltpu.VMEM((160, 6 * LANES), F32),
             pltpu.VMEM((128, 5 * LANES), BF16),
             pltpu.VMEM((LANES, LANES), F32),
-            pltpu.VMEM((8, LANES), F32),
-            pltpu.VMEM((group, 8, LANES), F32),
+            pltpu.VMEM((1, LANES), F32),
+            pltpu.VMEM((group, 1, LANES), F32),
             dma((KRYLOV, 3, 2)),
             dma((KRYLOV, 3, 2)),
             dma((2,)),

time: 30.2 us -> 29.5 us (0.977)
  Pallas kernels: 28.5 us -> 27.8 us
    pallas_call x1, Pallas kernels: 28.5 us -> 27.8 us  [local(): pl.pallas_call(functools.partial(kernel, sizes), out_shape=jax.ShapeDtype...]
where the time goes in v2:
time: 29.5 us; the launch traced here: 29.4 us
  Pallas kernels  27.8 us (94%)
  local copies, waits for them, and re-layouts  1.59 us (5%)
    pallas_call x1, Pallas kernels, local(): pl.pallas_call(functools.partial(kernel, sizes), out_shape=jax.ShapeDtype...  27.8 us
    unnamed x1, local copies, waits for them, and re-layouts  1.59 us

profile of v2, /device:TPU:0, one launch (start us, length us, event | category | flops | bytes accessed | tf_op | source)
XLA Modules:
  0.0 29.4 jit_solution(6263162078863453545)
XLA Ops:
  0.0 27.8 %shard_map.118 = f32[5,64,128]{2,1,0:T(8,128)} custom-call(f32[5,64,128]{2,1,0:T(8,128)} %bitcast.18, bf16[5,64,128]{2,1,0:T(8,128)(2,1)} %bitcast.19, bf16[3,5,5,64,128]{4,3,2,1,0:T(8,128)(2,1)} %bitcast.15, bf16[6,5,5,16,128]{4,3,2,1,0:T(8,128)(2,1)} %bitcast.17, s32[1,64]{1,0:T(1,128)} %bitcast.21, s32[1,64]{1,0:T(1,128)} %bitcast.22, s32[1,64]{1,0:T(1,128)} %bitcast.23, ...), custom_call_target="tpu_custom_call" | custom-call | tf_op jit(solution)/shard_map/pallas_call | solution.py:608
  27.8 1.6 %copy.15 = f32[5,4,4,4,1,1,128]{6,5,4,3,2,1,0:T(1,128)} copy(f32[5,4,4,4,1,1,128]{6,5,4,3,2,1,0:T(1,128)} %bitcast.16) | data formatting | bytes 327680

commit v3 on v2

--- a/solution.py
+++ b/solution.py
@@ -188,7 +188,20 @@
     has_low = [h > 0 for h in here]
     has_high = [h < n - 1 for h, n in zip(here, sizes)]
 
+    def wrapped(value, size):
+        return jnp.where(value >= size, value - size, value)
+
+    def each(action):
+        if group > 16:
+            pl.loop(1, group)(action)
+        else:
+            for step in range(1, group):
+                action(step)
+
     def peer(step):
+        if isinstance(step, int):
+            steps = (step // (sizes[1] * sizes[2]), step // sizes[2] % sizes[1], step % sizes[2])
+            return {a: wrapped(h + o, n) for a, h, o, n in zip(axes, here, steps, sizes)}
         other = lax.rem(me + step, group)
         return {
             "gx": other // (sizes[1] * sizes[2]),
@@ -198,9 +211,11 @@
 
     barrier = pltpu.get_barrier_semaphore()
 
-    @pl.loop(1, group)
-    def _(step):
-        pl.semaphore_signal(barrier, inc=1, device_id=peer(step), device_id_type=MESH)
+    each(
+        lambda step: pl.semaphore_signal(
+            barrier, inc=1, device_id=peer(step), device_id_type=MESH
+        )
+    )
 
     loads = [
         pltpu.make_async_copy(origin, target, load_sem.at[i])
@@ -456,8 +471,6 @@
             loads[11].wait()
 
         arrive(0, k)
-        arrive(1, k)
-        arrive(2, k)
         for s in range(2):
             for b in range(5):
                 put_trace(6 + s, b, halo_x[k, s, b])
@@ -496,6 +509,8 @@
         faces[...] = lax.dot_general(
             rows_left[...], place[...], (((1,), (1,)), ((), ())), preferred_element_type=F32
         )
+        arrive(1, k)
+        arrive(2, k)
         for f in range(6):
             d, s = f // 2, f % 2
             if d == 0:
@@ -531,7 +546,17 @@
         for a in range(5):
             xs[k + 1, a] = xs[k + 1, a] + added[:, a * LANES : (a + 1) * LANES]
 
-    products(KRYLOV, KRYLOV + 1)
+    last = [jnp.zeros((8, LANES), F32)] * (KRYLOV + 1)
+    for b in range(5):
+        for r in range(8):
+            at = slice(8 * r, 8 * r + 8)
+            newest = xs[KRYLOV, b, at]
+            for i in range(KRYLOV):
+                last[i] = last[i] + newest * xs[i, b, at]
+            last[KRYLOV] = last[KRYLOV] + newest * newest
+    for i in range(KRYLOV + 1):
+        row = KRYLOV * 8 + i
+        gram[row : row + 1] = jnp.sum(last[i], axis=0, keepdims=True)
     sums = lax.dot_general(
         jnp.ones((8, LANES), F32),
         gram[...],
@@ -551,24 +576,10 @@
             device_id_type=MESH,
         )
 
-    @pl.loop(1, group)
-    def _(step):
-        sum_copy(step).start()
-
+    each(lambda step: sum_copy(step).start())
     messages[0] = message[...]
-
-    @pl.loop(1, group)
-    def _(step):
-        sum_copy(step).wait_recv()
-
-    @pl.loop(1, group)
-    def _(step):
-        sum_copy(step).wait_send()
-
-    def add(i, total):
-        return total + messages[lax.rem(i + group - me, group)]
-
-    total = lax.fori_loop(0, group, add, jnp.zeros((1, LANES), F32))
+    each(lambda step: sum_copy(step).wait_recv())
+    total = jnp.sum(messages[...], axis=0)
     size = KRYLOV + 1
     entries = [[None] * size for _ in range(size)]
     for k in range(size):
@@ -584,6 +595,8 @@
             for k in range(1, KRYLOV):
                 value = value + scales[k] * xs[k, b, at]
             out[b, at] = value
+
+    each(lambda step: sum_copy(step).wait_send())
 
 
 def local(

time: 29.5 us -> 29 us (0.983)
  Pallas kernels: 27.8 us -> 27.2 us
    pallas_call x1, Pallas kernels: 27.8 us -> 27.2 us  [local(): pl.pallas_call(functools.partial(kernel, sizes), out_shape=jax.ShapeDtype...]
where the time goes in v3:
time: 29 us; the launch traced here: 28.8 us
  Pallas kernels  27.2 us (94%)
  local copies, waits for them, and re-layouts  1.59 us (5%)
    pallas_call x1, Pallas kernels, local(): pl.pallas_call(functools.partial(kernel, sizes), out_shape=jax.ShapeDtype...  27.2 us
    unnamed x1, local copies, waits for them, and re-layouts  1.59 us

profile of v3, /device:TPU:0, one launch (start us, length us, event | category | flops | bytes accessed | tf_op | source)
XLA Modules:
  0.0 28.8 jit_solution(17996745291123362055)
XLA Ops:
  0.0 27.2 %shard_map.118 = f32[5,64,128]{2,1,0:T(8,128)} custom-call(f32[5,64,128]{2,1,0:T(8,128)} %bitcast.18, bf16[5,64,128]{2,1,0:T(8,128)(2,1)} %bitcast.19, bf16[3,5,5,64,128]{4,3,2,1,0:T(8,128)(2,1)} %bitcast.15, bf16[6,5,5,16,128]{4,3,2,1,0:T(8,128)(2,1)} %bitcast.17, s32[1,64]{1,0:T(1,128)} %bitcast.21, s32[1,64]{1,0:T(1,128)} %bitcast.22, s32[1,64]{1,0:T(1,128)} %bitcast.23, ...), custom_call_target="tpu_custom_call" | custom-call | tf_op jit(solution)/shard_map/pallas_call | solution.py:621
  27.2 1.6 %copy.15 = f32[5,4,4,4,1,1,128]{6,5,4,3,2,1,0:T(1,128)} copy(f32[5,4,4,4,1,1,128]{6,5,4,3,2,1,0:T(1,128)} %bitcast.16) | data formatting | bytes 327680

commit v4 on v3

--- a/solution.py
+++ b/solution.py
@@ -251,14 +251,6 @@
                 if d == 0:
                     neighbour_pack[s] = jnp.full((32, LANES), -9.0, F32)
 
-    for load in loads[1:7]:
-        load.wait()
-    for half in range(2):
-        at = slice(64 * half, 64 * half + 64)
-        pack[0:25, at] = pairs[:, half, :]
-        for i in range(5):
-            pack[25 + i : 26 + i, at] = numbers[i].astype(F32)
-    pack[30:32] = jnp.zeros((2, LANES), F32)
     pl.semaphore_wait(barrier, group - 1)
 
     def to(d, s):
@@ -311,6 +303,16 @@
             def _(s=s):
                 face_copy(d, s, k).wait_send()
 
+    loads[0].wait()
+    start(0, 0)
+    for load in loads[1:7]:
+        load.wait()
+    for half in range(2):
+        at = slice(64 * half, 64 * half + 64)
+        pack[0:25, at] = pairs[:, half, :]
+        for i in range(5):
+            pack[25 + i : 26 + i, at] = numbers[i].astype(F32)
+    pack[30:32] = jnp.zeros((2, LANES), F32)
     for s in range(2):
 
         @pl.when(sides(0, s)[0])
@@ -400,11 +402,14 @@
             gram[pl.ds(k * 8 + i, 1), :] = jnp.sum(total, axis=0, keepdims=True)
 
     gram[...] = jnp.zeros_like(gram)
-    loads[0].wait()
 
     @pl.loop(0, KRYLOV)
     def _(k):
-        start(0, k)
+
+        @pl.when(k > 0)
+        def _():
+            start(0, k)
+
         for s in range(2):
             for b in range(5):
                 for i in range(4):

time: 29 us -> 29.1 us (level)
  no operation moved by 1% of the time
where the time goes in v4:
time: 29.1 us; the launch traced here: 29 us
  Pallas kernels  27.4 us (94%)
  local copies, waits for them, and re-layouts  1.59 us (5%)
    pallas_call x1, Pallas kernels, local(): pl.pallas_call(functools.partial(kernel, sizes), out_shape=jax.ShapeDtype...  27.4 us
    unnamed x1, local copies, waits for them, and re-layouts  1.59 us

profile of v4, /device:TPU:0, one launch (start us, length us, event | category | flops | bytes accessed | tf_op | source)
XLA Modules:
  0.0 29.0 jit_solution(17534342780574941639)
XLA Ops:
  0.0 27.4 %shard_map.118 = f32[5,64,128]{2,1,0:T(8,128)} custom-call(f32[5,64,128]{2,1,0:T(8,128)} %bitcast.18, bf16[5,64,128]{2,1,0:T(8,128)(2,1)} %bitcast.19, bf16[3,5,5,64,128]{4,3,2,1,0:T(8,128)(2,1)} %bitcast.15, bf16[6,5,5,16,128]{4,3,2,1,0:T(8,128)(2,1)} %bitcast.17, s32[1,64]{1,0:T(1,128)} %bitcast.21, s32[1,64]{1,0:T(1,128)} %bitcast.22, s32[1,64]{1,0:T(1,128)} %bitcast.23, ...), custom_call_target="tpu_custom_call" | custom-call | tf_op jit(solution)/shard_map/pallas_call | solution.py:626
  27.4 1.6 %copy.15 = f32[5,4,4,4,1,1,128]{6,5,4,3,2,1,0:T(1,128)} copy(f32[5,4,4,4,1,1,128]{6,5,4,3,2,1,0:T(1,128)} %bitcast.16) | data formatting | bytes 327680
